TPU v7x, 512 devices: a whole 4x8x8 slice. The times are simulated.
512 devices in a mesh: gx: 16 (over y, core), gy: 32 (over z, x).
Axes of the slice: x: 4, y: 8, z: 8, core: 2. Of those that a mesh axis runs over, the one named last changes fastest.
Arguments:
- counts: float32 [4, 256, 512, 512], P(None, 'gx', 'gy'), may hold values from -9000 to 9000, as said below
- spread: float32 [512], replicated, may hold values from 0.5 to 1.5
Outputs:
- scores: float32 [4, 256, 512, 512], P(None, 'gx', 'gy')
Inputs may be any that keep to these rules, and one draw needn't show every extreme that they name: Spectra of counts, real-valued; every entry is finite.
All inputs are finite; a program needn't handle non-finite values.
Results may differ from a plain program's by a relative error of at most 0.0003.
Values sent between devices are 32-bit elements; how exact they have to be, the bound alone decides.
A program may use at most 64 MiB of HBM per device.

v0:
```python
import math

import jax
import jax.numpy as jnp
from jax import lax
from jax.sharding import PartitionSpec as P

RADIUS = 2


def extended(array, sides, width):
    for axis, dim in sides:
        count, length = (lax.axis_size(axis), array.shape[dim])
        up = [(i, (i + 1) % count) for i in range(count - 1)]
        down = [(j, i) for i, j in up]
        last = lax.slice_in_dim(array, length - width, length, axis=dim)
        leading = lax.slice_in_dim(array, 0, width, axis=dim)
        before = lax.ppermute(last, axis, up)
        after = lax.ppermute(leading, axis, down)
        array = jnp.concatenate([before, array, after], axis=dim)
    return array


def from_partner(value, axis, distance):
    mask = 2**distance
    pairs = [(source, source ^ mask) for source in range(lax.axis_size(axis))]
    return lax.ppermute(value, axis, pairs)


def kernel_taps(spread):
    offsets = jnp.arange(-RADIUS, RADIUS + 1).astype(jnp.float32)[:, None]
    profile = jnp.exp(-offsets * offsets / (2.0 * spread[None, :] * spread[None, :]))
    return profile / jnp.sum(profile, axis=0, keepdims=True)


def blur_along(padded, taps, along, length):
    result = taps[0] * lax.slice_in_dim(padded, 0, length, axis=along)
    for shift_k in range(1, 2 * RADIUS + 1):
        result = result + taps[shift_k] * lax.slice_in_dim(
            padded, shift_k, shift_k + length, axis=along
        )
    return result


def local(counts, spread):
    taps = kernel_taps(spread)
    planes_here, rows_x, rows_y, bin_count = counts.shape
    padded = extended(counts, (("gx", 1), ("gy", 2)), RADIUS)
    first_pass = blur_along(padded, taps, 1, rows_x)
    smoothed = blur_along(first_pass, taps, 2, rows_y)
    local_rows = planes_here * rows_x * rows_y
    matrix_y = smoothed.reshape(local_rows, bin_count)
    gram_part = lax.dot_general(
        matrix_y,
        matrix_y,
        (((0,), (0,)), ((), ())),
        precision=lax.Precision.HIGHEST,
        preferred_element_type=jnp.float32,
    )
    reduced = gram_part
    for level in range(lax.axis_size("gx").bit_length() - 1):
        reduced = reduced + from_partner(reduced, "gx", level)
    for level in range(lax.axis_size("gy").bit_length() - 1):
        reduced = reduced + from_partner(reduced, "gy", level)
    lower = jnp.linalg.cholesky(reduced)
    identity = jnp.eye(bin_count, dtype=jnp.float32)
    lower_inv = lax.linalg.triangular_solve(lower, identity, left_side=True, lower=True)
    rows_all = local_rows * lax.axis_size("gx") * lax.axis_size("gy")
    scores = lax.dot_general(
        matrix_y,
        lower_inv,
        (((1,), (1,)), ((), ())),
        precision=lax.Precision.HIGHEST,
        preferred_element_type=jnp.float32,
    )
    scores = scores * math.sqrt(rows_all)
    return scores.reshape(planes_here, rows_x, rows_y, bin_count)


def solution(mesh):
    in_specs = (P(None, "gx", "gy", None), P())
    out_specs = P(None, "gx", "gy", None)
    return jax.shard_map(local, mesh=mesh, in_specs=in_specs, out_specs=out_specs, check_vma=False)
```

profile of v0, /device:TPU:29, one launch (start us, length us, event | category | flops | bytes accessed | tf_op | source)
XLA Modules:
  0.0 518.2 jit_solution(16020968664129098469)
XLA Ops:
  1.1 5.0 collective-permute-start
  6.1 1.9 collective-permute-start.1
  9.4 1.8 constant_dynamic-update-slice_fusion.1
  11.2 3.8 collective-permute-done.1
  15.4 2.8 collective-permute-start.2
  18.3 2.5 collective-permute-start.3
  20.8 4.3 collective-permute-done.2
  25.4 2.9 collective-permute-done.3
  29.4 2.1 fusion
  32.7 3.5 convolution_bitcast_fusion
  36.2 1.9 collective-permute-start.4
  38.1 2.6 collective-permute-done.4
  41.0 2.1 collective-permute-start.5
  43.1 24.4 %collective-permute-done.5 = f32[512,512]{0,1:T(8,128)S(1)} collective-permute-done((f32[512,512]{0,1:T(8,128)S(1)}, f32[512,512]{0,1:T(8,128)S(1)}, u32[]{:S(2)}, u32[]{:S(2)}) %collective-permute-start.5) | collective-permute-done | bytes 1048608 | tf_op jit(solution)/shard_map/ppermute | solution.py:27
  67.7 2.0 collective-permute-start.6
  69.7 48.3 %collective-permute-done.6 = f32[512,512]{0,1:T(8,128)S(1)} collective-permute-done((f32[512,512]{0,1:T(8,128)S(1)}, f32[512,512]{0,1:T(8,128)S(1)}, u32[]{:S(2)}, u32[]{:S(2)}) %collective-permute-start.6) | collective-permute-done | bytes 1048608 | tf_op jit(solution)/shard_map/ppermute | solution.py:27
  118.1 3.9 collective-permute-start.7
  122.0 48.3 %collective-permute-done.7 = f32[512,512]{0,1:T(8,128)S(1)} collective-permute-done((f32[512,512]{0,1:T(8,128)S(1)}, f32[512,512]{0,1:T(8,128)S(1)}, u32[]{:S(2)}, u32[]{:S(2)}) %collective-permute-start.7) | collective-permute-done | bytes 1048608 | tf_op jit(solution)/shard_map/ppermute | solution.py:27
  170.6 5.5 %collective-permute-start.8 = (f32[512,512]{0,1:T(8,128)S(1)}, f32[512,512]{0,1:T(8,128)S(1)}, u32[]{:S(2)}, u32[]{:S(2)}) collective-permute-start(f32[512,512]{0,1:T(8,128)S(1)} %add.110), channel_id=1, source_target_pairs={{0,1},{1,0},{2,3},{3,2},{4,5},{5,4},{6,7},{7,6},{8,9},{9,8},{10,11... | collective-permute-start | bytes 3145736 | tf_op jit(solution)/shard_map/ppermute | solution.py:27
  176.1 23.1 %collective-permute-done.8 = f32[512,512]{0,1:T(8,128)S(1)} collective-permute-done((f32[512,512]{0,1:T(8,128)S(1)}, f32[512,512]{0,1:T(8,128)S(1)}, u32[]{:S(2)}, u32[]{:S(2)}) %collective-permute-start.8) | collective-permute-done | bytes 1048608 | tf_op jit(solution)/shard_map/ppermute | solution.py:27
  199.4 1.9 collective-permute-start.9
  201.3 25.1 %collective-permute-done.9 = f32[512,512]{0,1:T(8,128)S(1)} collective-permute-done((f32[512,512]{0,1:T(8,128)S(1)}, f32[512,512]{0,1:T(8,128)S(1)}, u32[]{:S(2)}, u32[]{:S(2)}) %collective-permute-start.9) | collective-permute-done | bytes 1048608 | tf_op jit(solution)/shard_map/ppermute | solution.py:27
  226.6 4.0 collective-permute-start.10
  230.6 21.5 %collective-permute-done.10 = f32[512,512]{0,1:T(8,128)S(1)} collective-permute-done((f32[512,512]{0,1:T(8,128)S(1)}, f32[512,512]{0,1:T(8,128)S(1)}, u32[]{:S(2)}, u32[]{:S(2)}) %collective-permute-start.10) | collective-permute-done | bytes 1048608 | tf_op jit(solution)/shard_map/ppermute | solution.py:27
  252.3 8.2 %collective-permute-start.11 = (f32[512,512]{0,1:T(8,128)S(1)}, f32[512,512]{0,1:T(8,128)S(1)}, u32[]{:S(2)}, u32[]{:S(2)}) collective-permute-start(f32[512,512]{0,1:T(8,128)S(1)} %add.113), channel_id=1, source_target_pairs={{0,8},{1,9},{2,10},{3,11},{4,12},{5,13},{6,14},{7,15},{8,0},{9,1},... | collective-permute-start | bytes 3145736 | tf_op jit(solution)/shard_map/ppermute | solution.py:27
  260.6 45.1 %collective-permute-done.11 = f32[512,512]{0,1:T(8,128)S(1)} collective-permute-done((f32[512,512]{0,1:T(8,128)S(1)}, f32[512,512]{0,1:T(8,128)S(1)}, u32[]{:S(2)}, u32[]{:S(2)}) %collective-permute-start.11) | collective-permute-done | bytes 1048608 | tf_op jit(solution)/shard_map/ppermute | solution.py:27
  305.9 5.2 collective-permute-start.12
  313.1 46.2 %collective-permute-done.12 = f32[512,512]{0,1:T(8,128)} collective-permute-done((f32[512,512]{0,1:T(8,128)S(1)}, f32[512,512]{0,1:T(8,128)}, u32[]{:S(2)}, u32[]{:S(2)}) %collective-permute-start.12) | collective-permute-done | bytes 1048608 | tf_op jit(solution)/shard_map/ppermute | solution.py:27
  359.2 1.7 add.115
  361.0 1.3 copy.29
  362.3 1.4 fusion.15
  364.7 11.7 %cholesky.104 = f32[128,128]{1,0:T(8,128)S(1)} custom-call(f32[128,128]{1,0:T(8,128)S(1)} %cholesky.266), custom_call_target="Cholesky" | custom-call | tf_op jit(solution)/shard_map/jit(cholesky)/cholesky | solution.py:65
  376.6 9.8 %custom-call.30 = f32[1,128,128]{1,2,0:T(8,128)S(1)} custom-call(f32[1,128,128]{2,1,0:T(8,128)S(1)} %get-tuple-element.36), custom_call_target="InvertDiagBlocksLowerTriangular" | custom-call | tf_op jit(solution)/shard_map/jit(cholesky)/cholesky | solution.py:65
  388.9 11.7 %cholesky.217 = f32[128,128]{1,0:T(8,128)S(1)} custom-call(f32[128,128]{1,0:T(8,128)S(1)} %cholesky.270), custom_call_target="Cholesky" | custom-call | tf_op jit(solution)/shard_map/jit(cholesky)/cholesky | solution.py:65
  400.7 10.0 %custom-call.31 = f32[1,128,128]{1,2,0:T(8,128)S(1)} custom-call(f32[1,128,128]{2,1,0:T(8,128)S(1)} %get-tuple-element.33), custom_call_target="InvertDiagBlocksLowerTriangular" | custom-call | tf_op jit(solution)/shard_map/jit(cholesky)/cholesky | solution.py:65
  412.2 11.7 %cholesky.238 = f32[128,128]{1,0:T(8,128)S(1)} custom-call(f32[128,128]{1,0:T(8,128)S(1)} %cholesky.275), custom_call_target="Cholesky" | custom-call | tf_op jit(solution)/shard_map/jit(cholesky)/cholesky | solution.py:65
  424.6 9.8 %custom-call.32 = f32[1,128,128]{1,2,0:T(8,128)S(1)} custom-call(f32[1,128,128]{2,1,0:T(8,128)S(1)} %get-tuple-element.30), custom_call_target="InvertDiagBlocksLowerTriangular" | custom-call | tf_op jit(solution)/shard_map/jit(cholesky)/cholesky | solution.py:65
  435.8 11.9 %cholesky.255 = f32[128,128]{1,0:T(8,128)S(1)} custom-call(f32[128,128]{1,0:T(8,128)S(1)} %slice_subtract_fusion.2), custom_call_target="Cholesky" | custom-call | tf_op jit(solution)/shard_map/jit(cholesky)/cholesky | solution.py:65
  452.7 13.7 %while.1 = (s32[]{:T(128)}, f32[512,512]{1,0:T(8,128)}, s32[4,2]{0,1:T(2,128)S(1)}, f32[4,128,128]{2,1,0:T(8,128)}, s32[]{:T(128)}) while((s32[]{:T(128)}, f32[512,512]{1,0:T(8,128)}, s32[4,2]{0,1:T(2,128)S(1)}, f32[4,128,128]{2,1,0:T(8,128)}, s32[]{:T(128)}) %tuple.33), condition=%wide.while_cond, body=%wide.while_body.sunk | while | flops 2 | bytes 132705 | solution.py:67
  453.4 2.8 bitcast_dynamic-update-slice_fusion.2
  456.8 2.8 bitcast_dynamic-update-slice_fusion.2
  460.2 2.8 bitcast_dynamic-update-slice_fusion.2
  463.7 2.8 bitcast_dynamic-update-slice_fusion.2
  466.4 40.1 %custom-call.33 = f32[4,128,128]{1,2,0:T(8,128)S(1)} custom-call(f32[4,128,128]{2,1,0:T(8,128)} %get-tuple-element.12), custom_call_target="InvertDiagBlocksLowerTriangular" | custom-call | tf_op jit(solution)/shard_map/triangular_solve | solution.py:67
  507.6 1.4 convolution_subtract_fusion.1
  509.4 1.3 convolution_subtract_fusion
  511.2 1.6 convolution_subtract_fusion.2
  513.2 4.8 convolution_multiply_fusion
  (65 shorter events, 23.7 us)
Async XLA Ops:
  1.1 8.3 %collective-permute-start = (f32[4,2,16,512]{3,2,1,0:T(8,128)S(1)}, f32[4,2,16,512]{3,2,1,0:T(8,128)S(1)}, u32[]{:S(2)}, u32[]{:S(2)}) collective-permute-start(f32[4,2,16,512]{3,2,1,0:T(8,128)S(1)} %get-tuple-element.26), channel_id=1, source_target_pairs={{0,32},{32,64},{64,96},{96,128},{128,160},{160,192},{192,224},{224... | collective-permute-start | bytes 786440 | tf_op jit(solution)/shard_map/ppermute | solution.py:18
  6.1 8.9 %collective-permute-start.1 = (f32[4,2,16,512]{3,2,1,0:T(8,128)S(1)}, f32[4,2,16,512]{3,2,1,0:T(8,128)S(1)}, u32[]{:S(2)}, u32[]{:S(2)}) collective-permute-start(f32[4,2,16,512]{3,2,1,0:T(8,128)S(1)} %get-tuple-element.25), channel_id=1, source_target_pairs={{32,0},{64,32},{96,64},{128,96},{160,128},{192,160},{224,192},{256... | collective-permute-start | bytes 786440 | tf_op jit(solution)/shard_map/ppermute | solution.py:19
  15.4 9.8 %collective-permute-start.2 = (f32[4,20,2,512]{3,1,2,0:T(8,128)S(1)}, f32[4,20,2,512]{3,1,2,0:T(8,128)S(1)}, u32[]{:S(2)}, u32[]{:S(2)}) collective-permute-start(f32[4,20,2,512]{3,1,2,0:T(8,128)S(1)} %copy.23), channel_id=1, source_target_pairs={{0,1},{1,2},{2,3},{3,4},{4,5},{5,6},{6,7},{7,8},{8,9},{9,10},{10,1... | collective-permute-start | bytes 983048 | tf_op jit(solution)/shard_map/ppermute | solution.py:18
  18.3 10.1 %collective-permute-start.3 = (f32[4,20,2,512]{3,1,2,0:T(8,128)S(1)}, f32[4,20,2,512]{3,1,2,0:T(8,128)S(1)}, u32[]{:S(2)}, u32[]{:S(2)}) collective-permute-start(f32[4,20,2,512]{3,1,2,0:T(8,128)S(1)} %copy.24), channel_id=1, source_target_pairs={{1,0},{2,1},{3,2},{4,3},{5,4},{6,5},{7,6},{8,7},{9,8},{10,9},{11,1... | collective-permute-start | bytes 983048 | tf_op jit(solution)/shard_map/ppermute | solution.py:19
  36.2 4.6 collective-permute-start.4
  41.0 26.5 %collective-permute-start.5 = (f32[512,512]{0,1:T(8,128)S(1)}, f32[512,512]{0,1:T(8,128)S(1)}, u32[]{:S(2)}, u32[]{:S(2)}) collective-permute-start(f32[512,512]{0,1:T(8,128)S(1)} %add.107), channel_id=1, source_target_pairs={{0,64},{32,96},{64,0},{96,32},{128,192},{160,224},{192,128},{224,1... | collective-permute-start | bytes 3145736 | tf_op jit(solution)/shard_map/ppermute | solution.py:27
  67.7 50.2 %collective-permute-start.6 = (f32[512,512]{0,1:T(8,128)S(1)}, f32[512,512]{0,1:T(8,128)S(1)}, u32[]{:S(2)}, u32[]{:S(2)}) collective-permute-start(f32[512,512]{0,1:T(8,128)S(1)} %add.108), channel_id=1, source_target_pairs={{0,128},{32,160},{64,192},{96,224},{128,0},{160,32},{192,64},{224,... | collective-permute-start | bytes 3145736 | tf_op jit(solution)/shard_map/ppermute | solution.py:27
  118.1 52.2 %collective-permute-start.7 = (f32[512,512]{0,1:T(8,128)S(1)}, f32[512,512]{0,1:T(8,128)S(1)}, u32[]{:S(2)}, u32[]{:S(2)}) collective-permute-start(f32[512,512]{0,1:T(8,128)S(1)} %add.109), channel_id=1, source_target_pairs={{0,256},{32,288},{64,320},{96,352},{128,384},{160,416},{192,448},{... | collective-permute-start | bytes 3145736 | tf_op jit(solution)/shard_map/ppermute | solution.py:27
  170.6 28.6 %collective-permute-start.8 = (f32[512,512]{0,1:T(8,128)S(1)}, f32[512,512]{0,1:T(8,128)S(1)}, u32[]{:S(2)}, u32[]{:S(2)}) collective-permute-start(f32[512,512]{0,1:T(8,128)S(1)} %add.110), channel_id=1, source_target_pairs={{0,1},{1,0},{2,3},{3,2},{4,5},{5,4},{6,7},{7,6},{8,9},{9,8},{10,11... | collective-permute-start | bytes 3145736 | tf_op jit(solution)/shard_map/ppermute | solution.py:27
  199.4 27.0 %collective-permute-start.9 = (f32[512,512]{0,1:T(8,128)S(1)}, f32[512,512]{0,1:T(8,128)S(1)}, u32[]{:S(2)}, u32[]{:S(2)}) collective-permute-start(f32[512,512]{0,1:T(8,128)S(1)} %add.111), channel_id=1, source_target_pairs={{0,2},{1,3},{2,0},{3,1},{4,6},{5,7},{6,4},{7,5},{8,10},{9,11},{10,... | collective-permute-start | bytes 3145736 | tf_op jit(solution)/shard_map/ppermute | solution.py:27
  226.6 25.5 %collective-permute-start.10 = (f32[512,512]{0,1:T(8,128)S(1)}, f32[512,512]{0,1:T(8,128)S(1)}, u32[]{:S(2)}, u32[]{:S(2)}) collective-permute-start(f32[512,512]{0,1:T(8,128)S(1)} %add.112), channel_id=1, source_target_pairs={{0,4},{1,5},{2,6},{3,7},{4,0},{5,1},{6,2},{7,3},{8,12},{9,13},{10,... | collective-permute-start | bytes 3145736 | tf_op jit(solution)/shard_map/ppermute | solution.py:27
  252.3 53.4 %collective-permute-start.11 = (f32[512,512]{0,1:T(8,128)S(1)}, f32[512,512]{0,1:T(8,128)S(1)}, u32[]{:S(2)}, u32[]{:S(2)}) collective-permute-start(f32[512,512]{0,1:T(8,128)S(1)} %add.113), channel_id=1, source_target_pairs={{0,8},{1,9},{2,10},{3,11},{4,12},{5,13},{6,14},{7,15},{8,0},{9,1},... | collective-permute-start | bytes 3145736 | tf_op jit(solution)/shard_map/ppermute | solution.py:27
  305.9 7.1 %copy-start = (f32[512,512]{0,1:T(8,128)}, f32[512,512]{0,1:T(8,128)S(1)}, u32[]{:S(2)}) copy-start(f32[512,512]{0,1:T(8,128)S(1)} %add.114) | copy-start | bytes 3145732
  305.9 53.3 %collective-permute-start.12 = (f32[512,512]{0,1:T(8,128)S(1)}, f32[512,512]{0,1:T(8,128)}, u32[]{:S(2)}, u32[]{:S(2)}) collective-permute-start(f32[512,512]{0,1:T(8,128)S(1)} %add.114), channel_id=1, source_target_pairs={{0,16},{1,17},{2,18},{3,19},{4,20},{5,21},{6,22},{7,23},{8,24},{9,... | collective-permute-start | bytes 3145736 | tf_op jit(solution)/shard_map/ppermute | solution.py:27
  363.7 1.0 copy-start.2
  452.7 56.7 %copy-start.1 = (f32[512,512]{1,0:T(8,128)S(1)}, f32[512,512]{1,0:T(8,128)}, u32[]{:S(2)}) copy-start(f32[512,512]{1,0:T(8,128)} %fusion.24) | copy-start | bytes 3145732
where the time goes:
time: 528 us; the launch traced here: 518 us
  waiting for transfers between devices  296 us (56%)
  other arithmetic  132 us (25%)
  starting transfers between devices  46.8 us (9%)
  matrix products  20.4 us (4%)
  local copies, waits for them, and re-layouts  19.9 us (4%)
    ppermute x9, waiting for transfers between devices, from_partner(): return lax.ppermute(value, axis, pairs)  285 us
    another operation x14, other arithmetic, local(): lower = jnp.linalg.cholesky(reduced)  78.8 us
    another operation x3, other arithmetic, local(): lax.linalg.triangular_solve(lower, identity, left_side=True, lower=True)  41.2 us
    ppermute x9, starting transfers between devices, from_partner(): return lax.ppermute(value, axis, pairs)  34.7 us
    another operation x12, local copies, waits for them, and re-layouts  13.7 us
  transfers between devices with their start and end apart: 13, of which 13 were waited for; matrix products, arithmetic and copies ran while one was open for 1% of the time, Pallas kernels for 0%

commit v1 on v0

v1 whole, which is shorter than its diff:
```python
import math

import jax
import jax.numpy as jnp
from jax import lax
from jax.experimental import pallas as pl
from jax.experimental.pallas import tpu as pltpu
from jax.sharding import PartitionSpec as P

RADIUS = 2
BINS = 512
PLANES = 4
SIDE = 16
CORES = 2
X_CHIPS = 4
Y_CHIPS = 8
Z_CHIPS = 8
F32 = jnp.float32
BF16 = jnp.bfloat16
HIGHEST = lax.Precision.HIGHEST
MESH = pl.DeviceIdType.MESH

BLOCKS = [(i, j) for i in range(4) for j in range(i, 4)]
PACKED = len(BLOCKS) * 128
HALF = PACKED // CORES
QUARTER = HALF // X_CHIPS
EIGHTH = 24
PADDED = EIGHTH * Z_CHIPS
PANEL = 16


def split2(x):
    high = x.astype(BF16)
    return high, (x - high.astype(F32)).astype(BF16)


def split3(x):
    high = x.astype(BF16).astype(F32)
    rest = x - high
    middle = rest.astype(BF16).astype(F32)
    return high, middle, rest - middle


def tap_rows(spread):
    offsets = [float(k) for k in range(-RADIUS, RADIUS + 1)]
    profile = [jnp.exp(-k * k / (2.0 * spread * spread)) for k in offsets]
    total = profile[0]
    for row in profile[1:]:
        total = total + row
    return [row / total for row in profile]


def gram_kernel(
    counts_ref,
    spread_ref,
    gram_ref,
    smooth_ref,
    grid,
    blurred,
    smooth,
    edge_out,
    edge_in,
    corner_out,
    corner_in,
    packed,
    from_core,
    from_x,
    quarter,
    from_z,
    from_y,
    gathered,
    whole,
    load_sems,
    x_send,
    x_recv,
    y_send,
    y_recv,
    c_send,
    c_recv,
    red_send,
    red_recv,
    out_sems,
):
    gx, gy = lax.axis_index("gx"), lax.axis_index("gy")
    nx, ny = CORES * Y_CHIPS, Z_CHIPS * X_CHIPS
    core, y = lax.rem(gx, CORES), gx // CORES
    x, z = lax.rem(gy, X_CHIPS), gy // X_CHIPS

    loads = []
    for p in range(PLANES):
        load = pltpu.make_async_copy(
            counts_ref.at[p],
            grid.at[p, RADIUS : RADIUS + SIDE, 8 : 8 + SIDE, :],
            load_sems.at[p],
        )
        load.start()
        loads.append(load)

    def core_peer():
        return (y * CORES + 1 - core, gy)

    def x_peer(d):
        return (gx, z * X_CHIPS + lax.rem(x + d, X_CHIPS))

    def z_peer(d):
        return (gx, lax.rem(z + d, Z_CHIPS) * X_CHIPS + x)

    def y_peer(d):
        return (lax.rem(y + d, Y_CHIPS) * CORES + core, gy)

    def beside(dx, dy):
        return (lax.rem(gx + dx + nx, nx), lax.rem(gy + dy + ny, ny))

    around = [(dx, dy) for dx in (-1, 0, 1) for dy in (-1, 0, 1) if (dx, dy) != (0, 0)]
    partners = [beside(dx, dy) for dx, dy in around]
    partners += [core_peer()]
    partners += [x_peer(d) for d in range(1, X_CHIPS)]
    partners += [z_peer(d) for d in range(1, Z_CHIPS)]
    partners += [y_peer(d) for d in range(1, Y_CHIPS)]
    barrier = pltpu.get_barrier_semaphore()
    for partner in partners:
        pl.semaphore_signal(barrier, inc=1, device_id=partner, device_id_type=MESH)

    def there(dx, dy):
        inside = None
        for delta, here, size in ((dx, gx, nx), (dy, gy, ny)):
            if delta:
                test = here > 0 if delta < 0 else here < size - 1
                inside = test if inside is None else jnp.logical_and(inside, test)
        return inside

    for p in range(PLANES):
        loads[p].wait()
        for i in range(SIDE):
            row = grid[p, RADIUS + i, 8:16, :]
            edge_out[0, p, 2 * i : 2 * i + 2, :] = row[0:2]
            row2 = grid[p, RADIUS + i, 16:24, :]
            edge_out[1, p, 2 * i : 2 * i + 2, :] = row2[6:8]
        for a, first in ((0, 0), (1, SIDE - 2)):
            for b in (0, 1):
                corner_out[2 * a + b, 4 * p : 4 * p + 4, :] = edge_out[
                    b, p, 2 * first : 2 * first + 4, :
                ]

    pl.semaphore_wait(barrier, len(partners))

    def x_copy(p, side):
        rows = (RADIUS, RADIUS + SIDE - 2)[side]
        lands = (RADIUS + SIDE, 0)[side]
        return pltpu.make_async_remote_copy(
            src_ref=grid.at[p, rows : rows + 2, 8 : 8 + SIDE, :],
            dst_ref=grid.at[p, lands : lands + 2, 8 : 8 + SIDE, :],
            send_sem=x_send.at[p, side],
            recv_sem=x_recv.at[p, side],
            device_id=beside((-1, 1)[side], 0),
            device_id_type=MESH,
        )

    def y_copy(p, side):
        return pltpu.make_async_remote_copy(
            src_ref=edge_out.at[side, p],
            dst_ref=edge_in.at[1 - side, p],
            send_sem=y_send.at[p, side],
            recv_sem=y_recv.at[p, side],
            device_id=beside(0, (-1, 1)[side]),
            device_id_type=MESH,
        )

    def corner_copy(a, b):
        return pltpu.make_async_remote_copy(
            src_ref=corner_out.at[2 * a + b],
            dst_ref=corner_in.at[2 * (1 - a) + 1 - b],
            send_sem=c_send.at[2 * a + b],
            recv_sem=c_recv.at[2 * a + b],
            device_id=beside((-1, 1)[a], (-1, 1)[b]),
            device_id_type=MESH,
        )

    sign = (-1, 1)
    for a in (0, 1):
        for b in (0, 1):

            @pl.when(there(sign[a], sign[b]))
            def _():
                corner_copy(a, b).start()

            @pl.when(jnp.logical_not(there(sign[a], sign[b])))
            def _():
                corner_in[2 * a + b] = jnp.zeros((4 * PLANES, BINS), F32)

    for p in range(PLANES):
        for side in (0, 1):

            @pl.when(there(0, sign[side]))
            def _():
                y_copy(p, side).start()

            @pl.when(there(sign[side], 0))
            def _():
                x_copy(p, side).start()

    for side in (0, 1):

        @pl.when(jnp.logical_not(there(0, sign[side])))
        def _():
            edge_in[side] = jnp.zeros((PLANES, 2 * SIDE, BINS), F32)

        @pl.when(jnp.logical_not(there(sign[side], 0)))
        def _():
            lands = (0, RADIUS + SIDE)[side]
            for p in range(PLANES):
                grid[p, lands : lands + 2, 8 : 8 + SIDE, :] = jnp.zeros((2, SIDE, BINS), F32)

    taps = tap_rows(spread_ref[...])

    for a in (0, 1):
        for b in (0, 1):

            @pl.when(there(sign[1 - a], sign[1 - b]))
            def _():
                corner_copy(a, b).wait_recv()

    keeps = []
    for p in range(PLANES):
        for side in (0, 1):

            @pl.when(there(0, sign[1 - side]))
            def _():
                y_copy(p, side).wait_recv()

            @pl.when(there(sign[1 - side], 0))
            def _():
                x_copy(p, side).wait_recv()

        for b, lands in ((0, 6), (1, 8 + SIDE)):
            for i in range(SIDE):
                grid[p, RADIUS + i, lands : lands + 2, :] = edge_in[b, p, 2 * i : 2 * i + 2, :]
            for a, first in ((0, 0), (1, RADIUS + SIDE)):
                for i in (0, 1):
                    grid[p, first + i, lands : lands + 2, :] = corner_in[
                        2 * a + b, 4 * p + 2 * i : 4 * p + 2 * i + 2, :
                    ]

        def along_x(i, carry, p=p):
            for lo, hi in ((0, 8), (8, 24), (24, 32)):
                total = taps[0] * grid[p, i, lo:hi, :]
                for k in range(1, 2 * RADIUS + 1):
                    total = total + taps[k] * grid[p, i + k, lo:hi, :]
                blurred[i, lo:hi, :] = total
            return carry

        lax.fori_loop(0, SIDE, along_x, 0)

        def along_y(i, carry, p=p):
            total = taps[0] * blurred[i, 6 : 6 + SIDE, :]
            for k in range(1, 2 * RADIUS + 1):
                total = total + taps[k] * blurred[i, 6 + k : 6 + k + SIDE, :]
            at = pl.multiple_of(p * SIDE * SIDE + i * SIDE, SIDE)
            smooth[pl.ds(at, SIDE), :] = total
            return carry

        lax.fori_loop(0, SIDE, along_y, 0)
        rows = slice(p * SIDE * SIDE, (p + 1) * SIDE * SIDE)
        keep = pltpu.make_async_copy(smooth.at[rows], smooth_ref.at[rows], out_sems.at[p])
        keep.start()
        keeps.append(keep)

        high, low = split2(smooth[rows, :])
        left = jnp.concatenate([high, high, low], axis=0)
        right = jnp.concatenate([high, low, high], axis=0)
        at = 0
        for i in range(4):
            part = lax.dot_general(
                left[:, i * 128 : i * 128 + 128],
                right[:, i * 128 :],
                (((0,), (0,)), ((), ())),
                preferred_element_type=F32,
            )
            for j in range(4 - i):
                block = part[:, j * 128 : j * 128 + 128]
                if p == 0:
                    packed[at : at + 128, :] = block
                else:
                    packed[at : at + 128, :] += block
                at += 128

    def send(n, source, target, device):
        copy = pltpu.make_async_remote_copy(
            src_ref=source,
            dst_ref=target,
            send_sem=red_send.at[n],
            recv_sem=red_recv.at[n],
            device_id=device,
            device_id_type=MESH,
        )
        copy.start()
        return copy

    def rows_at(start, size):
        return pl.ds(pl.multiple_of(start, 8), size)

    sent = []
    copy = send(0, packed.at[rows_at((1 - core) * HALF, HALF)], from_core, core_peer())
    sent.append(copy)
    copy.wait_recv()
    mine = core * HALF
    packed[rows_at(mine, HALF), :] += from_core[...]

    copies = [
        send(
            d,
            packed.at[rows_at(mine + lax.rem(x + d, X_CHIPS) * QUARTER, QUARTER)],
            from_x.at[d - 1],
            x_peer(d),
        )
        for d in range(1, X_CHIPS)
    ]
    sent += copies
    quarter[QUARTER:PADDED, :] = jnp.zeros((PADDED - QUARTER, 128), F32)
    for copy in copies:
        copy.wait_recv()
    total = packed[rows_at(mine + x * QUARTER, QUARTER), :]
    for d in range(X_CHIPS - 1):
        total = total + from_x[d]
    quarter[0:QUARTER, :] = total

    copies = [
        send(
            3 + d,
            quarter.at[rows_at(lax.rem(z + d, Z_CHIPS) * EIGHTH, EIGHTH)],
            from_z.at[d - 1],
            z_peer(d),
        )
        for d in range(1, Z_CHIPS)
    ]
    sent += copies
    for copy in copies:
        copy.wait_recv()
    total = quarter[rows_at(z * EIGHTH, EIGHTH), :]
    for d in range(Z_CHIPS - 1):
        total = total + from_z[d]

    from_y[y] = total
    copies = [send(10 + d, from_y.at[y], from_y.at[y], y_peer(d)) for d in range(1, Y_CHIPS)]
    sent += copies
    for copy in copies:
        copy.wait_recv()
    total = from_y[0]
    for d in range(1, Y_CHIPS):
        total = total + from_y[d]

    here = rows_at(z * EIGHTH, EIGHTH)
    gathered[here, :] = total
    copies = [send(17 + d, gathered.at[here], gathered.at[here], z_peer(d)) for d in range(1, Z_CHIPS)]
    sent += copies
    for copy in copies:
        copy.wait_recv()

    here = rows_at(mine + x * QUARTER, QUARTER)
    copies = [
        send(24 + d, gathered.at[0:QUARTER], whole.at[here], x_peer(d)) for d in range(1, X_CHIPS)
    ]
    sent += copies
    whole[here, :] = gathered[0:QUARTER, :]
    for copy in copies:
        copy.wait_recv()

    here = rows_at(mine, HALF)
    copy = send(28, whole.at[here], whole.at[here], core_peer())
    sent.append(copy)
    copy.wait_recv()

    give = pltpu.make_async_copy(whole, gram_ref, out_sems.at[PLANES])
    give.start()
    for copy in sent:
        copy.wait_send()
    for p in range(PLANES):
        for side in (0, 1):

            @pl.when(there(0, sign[side]))
            def _():
                y_copy(p, side).wait_send()

            @pl.when(there(sign[side], 0))
            def _():
                x_copy(p, side).wait_send()

        keeps[p].wait()
    for a in (0, 1):
        for b in (0, 1):

            @pl.when(there(sign[a], sign[b]))
            def _():
                corner_copy(a, b).wait_send()

    give.wait()


def gram_call(counts, spread):
    dma = pltpu.SemaphoreType.DMA
    rows = PLANES * SIDE * SIDE
    return pl.pallas_call(
        gram_kernel,
        out_shape=[
            jax.ShapeDtypeStruct((PACKED, 128), F32),
            jax.ShapeDtypeStruct((rows, BINS), F32),
        ],
        in_specs=[
            pl.BlockSpec(memory_space=pl.ANY),
            pl.BlockSpec(memory_space=pltpu.VMEM),
        ],
        out_specs=[pl.BlockSpec(memory_space=pl.ANY)] * 2,
        scratch_shapes=[
            pltpu.VMEM((PLANES, SIDE + 2 * RADIUS, SIDE + 16, BINS), F32),
            pltpu.VMEM((SIDE, SIDE + 16, BINS), F32),
            pltpu.VMEM((rows, BINS), F32),
            pltpu.VMEM((2, PLANES, 2 * SIDE, BINS), F32),
            pltpu.VMEM((2, PLANES, 2 * SIDE, BINS), F32),
            pltpu.VMEM((4, 4 * PLANES, BINS), F32),
            pltpu.VMEM((4, 4 * PLANES, BINS), F32),
            pltpu.VMEM((PACKED, 128), F32),
            pltpu.VMEM((HALF, 128), F32),
            pltpu.VMEM((X_CHIPS - 1, QUARTER, 128), F32),
            pltpu.VMEM((PADDED, 128), F32),
            pltpu.VMEM((Z_CHIPS - 1, EIGHTH, 128), F32),
            pltpu.VMEM((Y_CHIPS, EIGHTH, 128), F32),
            pltpu.VMEM((PADDED, 128), F32),
            pltpu.VMEM((PACKED, 128), F32),
            dma((PLANES,)),
            dma((PLANES, 2)),
            dma((PLANES, 2)),
            dma((PLANES, 2)),
            dma((PLANES, 2)),
            dma((4,)),
            dma((4,)),
            dma((29,)),
            dma((29,)),
            dma((PLANES + 1,)),
        ],
        compiler_params=pltpu.CompilerParams(
            collective_id=0, has_side_effects=True, vmem_limit_bytes=48 << 20
        ),
    )(counts, spread)


def factor(a_ref, w_ref):
    sublane = lax.broadcasted_iota(jnp.int32, (8, 128), 0)
    lane = lax.broadcasted_iota(jnp.int32, (PANEL, 128), 1)

    def tile(s):
        return slice(s * 128, s * 128 + 128)

    def spread_row(value, i):
        return jnp.broadcast_to(value[i : i + 1, :], (8, 128))

    for t in range(4):
        block = tile(t)

        def panel(n, carry, t=t, block=block):
            here = pl.ds(pl.multiple_of(t * 128 + n * PANEL, PANEL), PANEL)
            tiles = [a_ref[here, tile(s)] for s in range(t, 4)]
            tiles += [w_ref[here, tile(s)] for s in range(t + 1)]
            corner = pltpu.roll(tiles[0], lax.rem(128 - n * PANEL, 128), axis=1)
            column = [
                [
                    jnp.broadcast_to(corner[8 * g : 8 * g + 8, j : j + 1], (8, 128))
                    for g in range(2)
                ]
                for j in range(PANEL)
            ]
            rows = [[value[0:8], value[8:16]] for value in tiles]
            pivots = [jnp.ones((8, 128), F32)] * 2
            for j in range(PANEL):
                h, q = divmod(j, 8)
                pivot = spread_row(column[j][h], q)
                inverse = pl.reciprocal(pivot, approx=False)
                pivots[h] = jnp.where(sublane == q, pivot, pivots[h])
                weight = [None, None]
                for g in range(h, 2):
                    weight[g] = column[j][g] * inverse
                    if g == h:
                        weight[g] = jnp.where(sublane > q, weight[g], 0.0)
                for i in range(j + 1, PANEL):
                    other = spread_row(column[i][h], q)
                    for g in range(h, 2):
                        column[i][g] = column[i][g] - (column[j][g] * other) * inverse
                for value in rows:
                    other = spread_row(value[h], q)
                    for g in range(h, 2):
                        value[g] = value[g] - weight[g] * other
            scale = [lax.rsqrt(value) for value in pivots]
            rows = [
                jnp.concatenate([value[0] * scale[0], value[1] * scale[1]], axis=0)
                for value in rows
            ]
            for m, s in enumerate(range(t, 4)):
                a_ref[here, tile(s)] = rows[m]
            for s in range(t + 1):
                w_ref[here, tile(s)] = rows[4 - t + s]
            high, middle, low = split3(jnp.where(lane >= (n + 1) * PANEL, rows[0], 0.0))
            left = jnp.concatenate([high, high, middle, high, low, middle], axis=0)
            high, middle, low = split3(jnp.concatenate(rows, axis=1))
            right = jnp.concatenate([high, middle, high, low, high, middle], axis=0)
            update = jnp.dot(
                left.T.astype(BF16), right.astype(BF16), preferred_element_type=F32
            )
            for m, s in enumerate(range(t, 4)):
                a_ref[block, tile(s)] -= update[:, tile(m)]
            for s in range(t + 1):
                w_ref[block, tile(s)] -= update[:, tile(4 - t + s)]
            return carry

        lax.fori_loop(0, 128 // PANEL, panel, 0)
        for s in range(t + 1, 4):
            left = a_ref[block, tile(s)].T
            a_ref[tile(s), s * 128 :] -= jnp.dot(
                left, a_ref[block, s * 128 :], precision=HIGHEST, preferred_element_type=F32
            )
            w_ref[tile(s), : (t + 1) * 128] -= jnp.dot(
                left, w_ref[block, : (t + 1) * 128], precision=HIGHEST, preferred_element_type=F32
            )


def whiten_kernel(scale, gram_ref, smooth_ref, scores_ref, a_ref, w_ref, smooth, scores, load_sem, out_sems):
    load = pltpu.make_async_copy(smooth_ref, smooth, load_sem)
    load.start()
    for n, (i, j) in enumerate(BLOCKS):
        a_ref[i * 128 : i * 128 + 128, j * 128 : j * 128 + 128] = gram_ref[n * 128 : n * 128 + 128, :]
    row = lax.broadcasted_iota(jnp.int32, (BINS, BINS), 0)
    column = lax.broadcasted_iota(jnp.int32, (BINS, BINS), 1)
    w_ref[...] = jnp.where(row == column, 1.0, 0.0).astype(F32)
    factor(a_ref, w_ref)
    load.wait()
    weights = w_ref[...] * scale
    high, low = split2(weights)
    top = jnp.concatenate([high[:256, :256], low[:256, :256], high[:256, :256]], axis=1)
    bottom = jnp.concatenate([high[256:], low[256:], high[256:]], axis=1)
    pieces = 4
    size = smooth.shape[0] // pieces
    copies = []
    for n in range(pieces):
        here = slice(n * size, (n + 1) * size)
        high, low = split2(smooth[here, :])
        left = jnp.concatenate([high[:, :256], high[:, :256], low[:, :256]], axis=1)
        scores[here, :256] = lax.dot_general(
            left, top, (((1,), (1,)), ((), ())), preferred_element_type=F32
        )
        left = jnp.concatenate([high, high, low], axis=1)
        scores[here, 256:] = lax.dot_general(
            left, bottom, (((1,), (1,)), ((), ())), preferred_element_type=F32
        )
        copy = pltpu.make_async_copy(scores.at[here], scores_ref.at[here], out_sems.at[n])
        copy.start()
        copies.append(copy)
    for copy in copies:
        copy.wait()


def whiten_call(gram, smooth, scale):
    rows = smooth.shape[0]

    def kernel(*refs):
        whiten_kernel(scale, *refs)

    return pl.pallas_call(
        kernel,
        out_shape=jax.ShapeDtypeStruct((rows, BINS), F32),
        in_specs=[
            pl.BlockSpec(memory_space=pltpu.VMEM),
            pl.BlockSpec(memory_space=pl.ANY),
        ],
        out_specs=pl.BlockSpec(memory_space=pl.ANY),
        scratch_shapes=[
            pltpu.VMEM((BINS, BINS), F32),
            pltpu.VMEM((BINS, BINS), F32),
            pltpu.VMEM((rows, BINS), F32),
            pltpu.VMEM((rows, BINS), F32),
            pltpu.SemaphoreType.DMA,
            pltpu.SemaphoreType.DMA((4,)),
        ],
        compiler_params=pltpu.CompilerParams(vmem_limit_bytes=48 << 20),
    )(gram, smooth)


def local(counts, spread):
    gram, smooth = gram_call(counts, spread.reshape(1, BINS))
    rows_all = smooth.shape[0] * lax.axis_size("gx") * lax.axis_size("gy")
    scores = whiten_call(gram, smooth, math.sqrt(rows_all))
    return scores.reshape(counts.shape)


def solution(mesh):
    in_specs = (P(None, "gx", "gy", None), P())
    out_specs = P(None, "gx", "gy", None)
    return jax.shard_map(local, mesh=mesh, in_specs=in_specs, out_specs=out_specs, check_vma=False)
```

time: 528 us -> 84.4 us (0.16)
  the two profiles are of different devices: /device:TPU:29 before, /device:TPU:1 now
where the time goes in v1:
time: 84.4 us; the launch traced here: 84.2 us
  Pallas kernels  82 us (97%)
  local copies, waits for them, and re-layouts  2.27 us (3%)
    pallas_call x1, Pallas kernels, gram_call(): pl.pallas_call(gram_kernel, out_shape=[jax.ShapeDtypeStruct((PACKED, 128)...  58.1 us
    pallas_call x1, Pallas kernels, whiten_call(): pl.pallas_call(kernel, out_shape=jax.ShapeDtypeStruct((rows, BINS), F32),...  23.8 us
    unnamed x4, local copies, waits for them, and re-layouts  2.27 us

profile of v1, /device:TPU:1, one launch (start us, length us, event | category | flops | bytes accessed | tf_op | source)
XLA Modules:
  0.0 84.2 jit_solution(11456318082802428720)
XLA Ops:
  0.0 0.0 copy-start
  0.0 1.6 %copy-done = f32[4,16,16,512]{3,2,1,0:T(8,128)S(1)} copy-done((f32[4,16,16,512]{3,2,1,0:T(8,128)S(1)}, f32[4,16,16,512]{3,2,1,0:T(8,128)}, u32[]{:S(2)}) %copy-start) | copy-done | bytes 2097176
  1.6 0.0 copy-start.1
  1.6 0.7 copy-done.1
  2.3 58.1 %shard_map.28 = (f32[1280,128]{1,0:T(8,128)S(1)}, f32[1024,512]{1,0:T(8,128)S(1)}) custom-call(f32[4,16,16,512]{3,2,1,0:T(8,128)S(1)} %copy-done, f32[1,512]{1,0:T(1,128)S(1)} %bitcast.2), custom_call_target="tpu_custom_call" | custom-call | tf_op jit(solution)/shard_map/pallas_call | solution.py:402
  60.4 23.8 %shard_map.29 = f32[1024,512]{1,0:T(8,128)} custom-call(f32[1280,128]{1,0:T(8,128)S(1)} %get-tuple-element.7.refs_0_, f32[1024,512]{1,0:T(8,128)S(1)} %get-tuple-element.8.refs_1_), custom_call_target="tpu_custom_call" | custom-call | tf_op jit(solution)/shard_map/pallas_call | solution.py:565
Async XLA Ops:
  0.0 1.6 %copy-start = (f32[4,16,16,512]{3,2,1,0:T(8,128)S(1)}, f32[4,16,16,512]{3,2,1,0:T(8,128)}, u32[]{:S(2)}) copy-start(f32[4,16,16,512]{3,2,1,0:T(8,128)} %counts_ref.1) | copy-start | bytes 6291460
  1.6 0.7 copy-start.1

commit v2 on v1

v2 whole, which is shorter than its diff:
```python
import functools
import math

import jax
import jax.numpy as jnp
from jax import lax
from jax.experimental import pallas as pl
from jax.experimental.pallas import tpu as pltpu
from jax.sharding import PartitionSpec as P

RADIUS = 2
BINS = 512
PLANES = 4
SIDE = 16
CORES = 2
X_CHIPS = 4
Y_CHIPS = 8
Z_CHIPS = 8
F32 = jnp.float32
BF16 = jnp.bfloat16
MESH = pl.DeviceIdType.MESH

BLOCKS = [(i, j) for i in range(4) for j in range(i, 4)]
PACKED = len(BLOCKS) * 128
CHUNKS = [(0, 512), (512, PACKED - 512)]


def shares(rows):
    half = rows // CORES
    quarter = half // X_CHIPS
    eighth = -(-quarter // (8 * Z_CHIPS)) * 8
    return half, quarter, eighth


PANEL = 16
PIECES = 8


def split3(x):
    high = x.astype(BF16)
    rest = x - high.astype(F32)
    middle = rest.astype(BF16)
    return high, middle, (rest - middle.astype(F32)).astype(BF16)


def left_parts(x, axis):
    high, middle, low = split3(x)
    return jnp.concatenate([high, high, middle, high, low, middle], axis=axis)


def right_parts(x, axis):
    high, middle, low = split3(x)
    return jnp.concatenate([high, middle, high, low, high, middle], axis=axis)


def tile(s):
    return slice(s * 128, s * 128 + 128)


def dot(left, right):
    return jnp.dot(left, right, preferred_element_type=F32)


def tap_rows(spread):
    offsets = [float(k) for k in range(-RADIUS, RADIUS + 1)]
    profile = [jnp.exp(-k * k / (2.0 * spread * spread)) for k in offsets]
    total = profile[0]
    for row in profile[1:]:
        total = total + row
    return [row / total for row in profile]


def gram_kernel(
    counts_ref,
    spread_ref,
    gram_ref,
    smooth_ref,
    grid,
    blurred,
    smooth,
    edge_out,
    edge_in,
    corner_out,
    corner_in,
    packed,
    from_core0,
    from_x0,
    quarter0,
    from_z0,
    from_y0,
    gathered0,
    from_core1,
    from_x1,
    quarter1,
    from_z1,
    from_y1,
    gathered1,
    whole,
    taps_in,
    load_sems,
    taps_sem,
    x_send,
    x_recv,
    y_send,
    y_recv,
    c_send,
    c_recv,
    red_send,
    red_recv,
    out_sems,
):
    gx, gy = lax.axis_index("gx"), lax.axis_index("gy")
    nx, ny = CORES * Y_CHIPS, Z_CHIPS * X_CHIPS
    core, y = lax.rem(gx, CORES), gx // CORES
    x, z = lax.rem(gy, X_CHIPS), gy // X_CHIPS

    taps_load = pltpu.make_async_copy(spread_ref, taps_in, taps_sem)
    taps_load.start()
    loads = []
    for p in range(PLANES):
        load = pltpu.make_async_copy(
            counts_ref.at[p],
            grid.at[p, RADIUS : RADIUS + SIDE, 8 : 8 + SIDE, :],
            load_sems.at[p],
        )
        load.start()
        loads.append(load)

    def core_peer():
        return (y * CORES + 1 - core, gy)

    def x_peer(d):
        return (gx, z * X_CHIPS + lax.rem(x + d, X_CHIPS))

    def z_peer(d):
        return (gx, lax.rem(z + d, Z_CHIPS) * X_CHIPS + x)

    def y_peer(d):
        return (lax.rem(y + d, Y_CHIPS) * CORES + core, gy)

    def beside(dx, dy):
        return (lax.rem(gx + dx + nx, nx), lax.rem(gy + dy + ny, ny))

    around = [(dx, dy) for dx in (-1, 0, 1) for dy in (-1, 0, 1) if (dx, dy) != (0, 0)]
    partners = [beside(dx, dy) for dx, dy in around]
    partners += [core_peer()]
    partners += [x_peer(d) for d in range(1, X_CHIPS)]
    partners += [z_peer(d) for d in range(1, Z_CHIPS)]
    partners += [y_peer(d) for d in range(1, Y_CHIPS)]
    barrier = pltpu.get_barrier_semaphore()
    for partner in partners:
        pl.semaphore_signal(barrier, inc=1, device_id=partner, device_id_type=MESH)

    def there(dx, dy):
        inside = None
        for delta, here, size in ((dx, gx, nx), (dy, gy, ny)):
            if delta:
                test = here > 0 if delta < 0 else here < size - 1
                inside = test if inside is None else jnp.logical_and(inside, test)
        return inside

    for p in range(PLANES):
        loads[p].wait()
        for i in range(SIDE):
            row = grid[p, RADIUS + i, 8:16, :]
            edge_out[0, p, 2 * i : 2 * i + 2, :] = row[0:2]
            row2 = grid[p, RADIUS + i, 16:24, :]
            edge_out[1, p, 2 * i : 2 * i + 2, :] = row2[6:8]
        for a, first in ((0, 0), (1, SIDE - 2)):
            for b in (0, 1):
                corner_out[2 * a + b, 4 * p : 4 * p + 4, :] = edge_out[
                    b, p, 2 * first : 2 * first + 4, :
                ]

    pl.semaphore_wait(barrier, len(partners))

    def x_copy(p, side):
        rows = (RADIUS, RADIUS + SIDE - 2)[side]
        lands = (RADIUS + SIDE, 0)[side]
        return pltpu.make_async_remote_copy(
            src_ref=grid.at[p, rows : rows + 2, 8 : 8 + SIDE, :],
            dst_ref=grid.at[p, lands : lands + 2, 8 : 8 + SIDE, :],
            send_sem=x_send.at[p, side],
            recv_sem=x_recv.at[p, side],
            device_id=beside((-1, 1)[side], 0),
            device_id_type=MESH,
        )

    def y_copy(p, side):
        return pltpu.make_async_remote_copy(
            src_ref=edge_out.at[side, p],
            dst_ref=edge_in.at[1 - side, p],
            send_sem=y_send.at[p, side],
            recv_sem=y_recv.at[p, side],
            device_id=beside(0, (-1, 1)[side]),
            device_id_type=MESH,
        )

    def corner_copy(a, b):
        return pltpu.make_async_remote_copy(
            src_ref=corner_out.at[2 * a + b],
            dst_ref=corner_in.at[2 * (1 - a) + 1 - b],
            send_sem=c_send.at[2 * a + b],
            recv_sem=c_recv.at[2 * a + b],
            device_id=beside((-1, 1)[a], (-1, 1)[b]),
            device_id_type=MESH,
        )

    sign = (-1, 1)
    for a in (0, 1):
        for b in (0, 1):

            @pl.when(there(sign[a], sign[b]))
            def _():
                corner_copy(a, b).start()

            @pl.when(jnp.logical_not(there(sign[a], sign[b])))
            def _():
                corner_in[2 * a + b] = jnp.zeros((4 * PLANES, BINS), F32)

    for p in range(PLANES):
        for side in (0, 1):

            @pl.when(there(0, sign[side]))
            def _():
                y_copy(p, side).start()

            @pl.when(there(sign[side], 0))
            def _():
                x_copy(p, side).start()

    for side in (0, 1):

        @pl.when(jnp.logical_not(there(0, sign[side])))
        def _():
            edge_in[side] = jnp.zeros((PLANES, 2 * SIDE, BINS), F32)

        @pl.when(jnp.logical_not(there(sign[side], 0)))
        def _():
            lands = (0, RADIUS + SIDE)[side]
            for p in range(PLANES):
                grid[p, lands : lands + 2, 8 : 8 + SIDE, :] = jnp.zeros((2, SIDE, BINS), F32)

    taps_load.wait()
    taps = tap_rows(taps_in[...])

    for a in (0, 1):
        for b in (0, 1):

            @pl.when(there(sign[1 - a], sign[1 - b]))
            def _():
                corner_copy(a, b).wait_recv()

    def rows_at(start, size):
        return pl.ds(pl.multiple_of(start, 8), size)

    buffers = [
        (from_core0, from_x0, quarter0, from_z0, from_y0, gathered0),
        (from_core1, from_x1, quarter1, from_z1, from_y1, gathered1),
    ]
    sent = []
    gives = []

    def reduction(c):
        first, rows = CHUNKS[c]
        half, fourth, eighth = shares(rows)
        from_core, from_x, quarter, from_z, from_y, gathered = buffers[c]

        def send(n, source, target, device):
            copy = pltpu.make_async_remote_copy(
                src_ref=source,
                dst_ref=target,
                send_sem=red_send.at[c, n],
                recv_sem=red_recv.at[c, n],
                device_id=device,
                device_id_type=MESH,
            )
            copy.start()
            sent.append(copy)
            return copy

        copy = send(
            0, packed.at[rows_at(first + (1 - core) * half, half)], from_core, core_peer()
        )
        if fourth < Z_CHIPS * eighth:
            quarter[fourth:, :] = jnp.zeros((Z_CHIPS * eighth - fourth, 128), F32)
        yield
        copy.wait_recv()
        mine = first + core * half
        packed[rows_at(mine, half), :] += from_core[...]

        copies = [
            send(
                d,
                packed.at[rows_at(mine + lax.rem(x + d, X_CHIPS) * fourth, fourth)],
                from_x.at[d - 1],
                x_peer(d),
            )
            for d in range(1, X_CHIPS)
        ]
        yield
        for copy in copies:
            copy.wait_recv()
        total = packed[rows_at(mine + x * fourth, fourth), :]
        for d in range(X_CHIPS - 1):
            total = total + from_x[d]
        quarter[0:fourth, :] = total

        copies = [
            send(
                3 + d,
                quarter.at[rows_at(lax.rem(z + d, Z_CHIPS) * eighth, eighth)],
                from_z.at[d - 1],
                z_peer(d),
            )
            for d in range(1, Z_CHIPS)
        ]
        yield
        for copy in copies:
            copy.wait_recv()
        total = quarter[rows_at(z * eighth, eighth), :]
        for d in range(Z_CHIPS - 1):
            total = total + from_z[d]

        from_y[y] = total
        copies = [send(10 + d, from_y.at[y], from_y.at[y], y_peer(d)) for d in range(1, Y_CHIPS)]
        yield
        for copy in copies:
            copy.wait_recv()
        total = from_y[0]
        for d in range(1, Y_CHIPS):
            total = total + from_y[d]

        here = rows_at(z * eighth, eighth)
        gathered[here, :] = total
        copies = [
            send(17 + d, gathered.at[here], gathered.at[here], z_peer(d))
            for d in range(1, Z_CHIPS)
        ]
        yield
        for copy in copies:
            copy.wait_recv()
        here = rows_at(mine + x * fourth, fourth)
        copies = [
            send(24 + d, gathered.at[0:fourth], whole.at[here], x_peer(d))
            for d in range(1, X_CHIPS)
        ]
        whole[here, :] = gathered[0:fourth, :]
        yield
        for copy in copies:
            copy.wait_recv()
        here = rows_at(mine, half)
        copy = send(28, whole.at[here], whole.at[here], core_peer())
        yield
        copy.wait_recv()
        give = pltpu.make_async_copy(
            whole.at[first : first + rows], gram_ref.at[first : first + rows], out_sems.at[PLANES + c]
        )
        give.start()
        gives.append(give)

    keeps = []
    for p in range(PLANES):
        for side in (0, 1):

            @pl.when(there(0, sign[1 - side]))
            def _():
                y_copy(p, side).wait_recv()

            @pl.when(there(sign[1 - side], 0))
            def _():
                x_copy(p, side).wait_recv()

        for b, lands in ((0, 6), (1, 8 + SIDE)):
            for i in range(SIDE):
                grid[p, RADIUS + i, lands : lands + 2, :] = edge_in[b, p, 2 * i : 2 * i + 2, :]
            for a, first in ((0, 0), (1, RADIUS + SIDE)):
                for i in (0, 1):
                    grid[p, first + i, lands : lands + 2, :] = corner_in[
                        2 * a + b, 4 * p + 2 * i : 4 * p + 2 * i + 2, :
                    ]

        def along_x(i, carry, p=p):
            for lo, hi in ((0, 8), (8, 24), (24, 32)):
                total = taps[0] * grid[p, i, lo:hi, :]
                for k in range(1, 2 * RADIUS + 1):
                    total = total + taps[k] * grid[p, i + k, lo:hi, :]
                blurred[i, lo:hi, :] = total
            return carry

        lax.fori_loop(0, SIDE, along_x, 0)

        def along_y(i, carry, p=p):
            total = taps[0] * blurred[i, 6 : 6 + SIDE, :]
            for k in range(1, 2 * RADIUS + 1):
                total = total + taps[k] * blurred[i, 6 + k : 6 + k + SIDE, :]
            at = pl.multiple_of(p * SIDE * SIDE + i * SIDE, SIDE)
            smooth[pl.ds(at, SIDE), :] = total
            return carry

        lax.fori_loop(0, SIDE, along_y, 0)
        rows = slice(p * SIDE * SIDE, (p + 1) * SIDE * SIDE)
        keep = pltpu.make_async_copy(smooth.at[rows], smooth_ref.at[rows], out_sems.at[p])
        keep.start()
        keeps.append(keep)

        value = smooth[rows, :]
        left = left_parts(value.T, 1)
        right = right_parts(value, 0)
        at = 0
        for i in range(4):
            part = dot(left[tile(i), :], right[:, i * 128 :])
            for j in range(4 - i):
                block = part[:, tile(j)]
                if p == 0:
                    packed[at : at + 128, :] = block
                else:
                    packed[at : at + 128, :] += block
                at += 128
            if p == PLANES - 1 and i == 0:
                first_chunk = reduction(0)
                next(first_chunk)

    second_chunk = reduction(1)
    next(second_chunk)
    under_way = [first_chunk, second_chunk]
    while under_way:
        under_way = [chunk for chunk in under_way if next(chunk, chunk) is not chunk]
    for copy in sent:
        copy.wait_send()
    for p in range(PLANES):
        for side in (0, 1):

            @pl.when(there(0, sign[side]))
            def _():
                y_copy(p, side).wait_send()

            @pl.when(there(sign[side], 0))
            def _():
                x_copy(p, side).wait_send()

        keeps[p].wait()
    for a in (0, 1):
        for b in (0, 1):

            @pl.when(there(sign[a], sign[b]))
            def _():
                corner_copy(a, b).wait_send()

    for give in gives:
        give.wait()


def gram_call(counts, spread):
    dma = pltpu.SemaphoreType.DMA
    rows = PLANES * SIDE * SIDE
    reduction_buffers = []
    for _, chunk in CHUNKS:
        half, fourth, eighth = shares(chunk)
        for shape in (
            (half,),
            (X_CHIPS - 1, fourth),
            (Z_CHIPS * eighth,),
            (Z_CHIPS - 1, eighth),
            (Y_CHIPS, eighth),
            (Z_CHIPS * eighth,),
        ):
            reduction_buffers.append(pltpu.VMEM((*shape, 128), F32))
    return pl.pallas_call(
        gram_kernel,
        out_shape=[
            jax.ShapeDtypeStruct((PACKED, 128), F32),
            jax.ShapeDtypeStruct((rows, BINS), F32),
        ],
        in_specs=[pl.BlockSpec(memory_space=pl.ANY)] * 2,
        out_specs=[pl.BlockSpec(memory_space=pl.ANY)] * 2,
        scratch_shapes=[
            pltpu.VMEM((PLANES, SIDE + 2 * RADIUS, SIDE + 16, BINS), F32),
            pltpu.VMEM((SIDE, SIDE + 16, BINS), F32),
            pltpu.VMEM((rows, BINS), F32),
            pltpu.VMEM((2, PLANES, 2 * SIDE, BINS), F32),
            pltpu.VMEM((2, PLANES, 2 * SIDE, BINS), F32),
            pltpu.VMEM((4, 4 * PLANES, BINS), F32),
            pltpu.VMEM((4, 4 * PLANES, BINS), F32),
            pltpu.VMEM((PACKED, 128), F32),
            *reduction_buffers,
            pltpu.VMEM((PACKED, 128), F32),
            pltpu.VMEM((1, BINS), F32),
            dma((PLANES,)),
            dma,
            dma((PLANES, 2)),
            dma((PLANES, 2)),
            dma((PLANES, 2)),
            dma((PLANES, 2)),
            dma((4,)),
            dma((4,)),
            dma((2, 29)),
            dma((2, 29)),
            dma((PLANES + 2,)),
        ],
        compiler_params=pltpu.CompilerParams(
            collective_id=0, has_side_effects=True, vmem_limit_bytes=62 << 20
        ),
    )(counts, spread)


def factor_block(t, a_ref, w_ref, parts_ref, work):
    sublane = lax.broadcasted_iota(jnp.int32, (8, 128), 0)
    panels = 128 // PANEL
    width = 4 - t

    def at(s, rows):
        return (a_ref, rows, tile(t + s)) if s < width else (w_ref, rows, slice(0, 128))

    def column_parts(value, first, keep):
        lane = lax.broadcasted_iota(jnp.int32, value.shape, 1)
        column = jnp.take_along_axis(value, first + lane % PANEL, axis=1)
        if keep is not None:
            column = jnp.where(keep, column, 0.0)
        high, middle, low = split3(column)
        high, middle, low = high.astype(F32), middle.astype(F32), low.astype(F32)
        group = lane // PANEL
        value = jnp.where(
            (group == 0) | (group == 1) | (group == 3),
            high,
            jnp.where((group == 2) | (group == 5), middle, jnp.where(group == 4, low, 0.0)),
        )
        return value.astype(BF16)

    def lose(rows, left, right):
        update = dot(left, right)
        for s in range(width + 1):
            ref, at_rows, columns = at(s, rows)
            ref[at_rows, columns] -= update[:, tile(s)]

    for p in range(panels):
        first = t * 128 + p * PANEL
        here = slice(first, first + PANEL)
        rows = []
        for s in range(width + 1):
            ref, at_rows, columns = at(s, here)
            rows.append([ref[first + 8 * g : first + 8 * g + 8, columns] for g in range(2)])
        column = [
            [
                jnp.take_along_axis(
                    rows[0][g], jnp.full((8, 128), p * PANEL + j, jnp.int32), axis=1
                )
                for g in range(2)
            ]
            for j in range(PANEL)
        ]
        factor = [list(value) for value in rows]
        pivots = [jnp.ones((8, 128), F32)] * 2
        inverses = [jnp.ones((8, 128), F32)] * 2
        if 0 < p < panels - 1:
            beyond = slice(first + PANEL, t * 128 + 128)
            left = column_parts(a_ref[beyond, tile(t)], (p - 1) * PANEL, None)
            lose(beyond, left, parts_ref[:, : (width + 1) * 128])
        for j in range(PANEL):
            h, q = divmod(j, 8)
            pivot = jnp.broadcast_to(column[j][h][q : q + 1, :], (8, 128))
            inverse = 1.0 / pivot
            pivots[h] = jnp.where(sublane == q, pivot, pivots[h])
            inverses[h] = jnp.where(sublane == q, inverse, inverses[h])
            weight = [
                (jnp.where(sublane != q, column[j][g], 0.0) if g == h else column[j][g]) * inverse
                for g in range(2)
            ]
            for i in range(j + 1, PANEL):
                other = jnp.broadcast_to(column[i][h][q : q + 1, :], (8, 128))
                for g in range(2):
                    column[i][g] = column[i][g] - weight[g] * other
            for value, kept in zip(rows, factor):
                other = jnp.broadcast_to(value[h][q : q + 1, :], (8, 128))
                kept[h] = jnp.where(sublane == q, other, kept[h])
                for g in range(2):
                    value[g] = value[g] - weight[g] * other
            if j in (3, 9) and work:
                work.pop(0)()
        scale = [lax.rsqrt(value) for value in pivots]
        for s, kept in enumerate(factor):
            ref, at_rows, columns = at(s, here)
            ref[at_rows, columns] = jnp.concatenate([kept[g] * scale[g] for g in range(2)], axis=0)
        if p < panels - 1:
            solved = jnp.concatenate(
                [
                    jnp.concatenate([value[g] * inverses[g] for g in range(2)], axis=0)
                    for value in rows
                ],
                axis=1,
            )
            right = right_parts(solved, 0)
            right = jnp.concatenate([right, jnp.zeros((128 - 6 * PANEL, right.shape[1]), BF16)], axis=0)
            parts_ref[:, : (width + 1) * 128] = right
            after = slice(first + PANEL, first + 2 * PANEL)
            lose(after, column_parts(a_ref[after, tile(t)], p * PANEL, None), right)
    while work:
        work.pop(0)()


def whiten_kernel(
    scale, gram_ref, smooth_ref, scores_ref, a_ref, w_ref, parts_ref, wp_ref, up_ref, left_ref, scores, load_sem, out_sems
):
    load = pltpu.make_async_copy(smooth_ref, left_ref, load_sem)
    load.start()
    for n, (i, j) in enumerate(BLOCKS):
        a_ref[tile(i), tile(j)] = gram_ref[tile(n), :]
    size = left_ref.shape[0] // PIECES
    copies = []

    def solve(t, n):
        here = slice(n * size, (n + 1) * size)
        value = lax.dot_general(
            left_parts(left_ref[here, tile(t)], 1),
            wp_ref[t],
            (((1,), (1,)), ((), ())),
            preferred_element_type=F32,
        )
        scores[here, tile(t)] = value * scale
        if t < 3:
            behind = (3 - t) * 128
            left_ref[here, (t + 1) * 128 :] -= dot(left_parts(value, 1), up_ref[t, :, :behind])
        copy = pltpu.make_async_copy(
            scores.at[here, tile(t)], scores_ref.at[here, tile(t)], out_sems.at[t, n]
        )
        copy.start()
        copies.append(copy)

    row = lax.broadcasted_iota(jnp.int32, (128, 128), 0)
    lane = lax.broadcasted_iota(jnp.int32, (128, 128), 1)
    identity = jnp.where(row == lane, 1.0, 0.0).astype(F32)
    work = []
    for t in range(4):
        w_ref[tile(t), :] = identity
        factor_block(t, a_ref, w_ref, parts_ref, work)
        if t == 0:
            load.wait()
        wp_ref[t] = right_parts(w_ref[tile(t), :], 1)
        if t < 3:
            behind = (3 - t) * 128
            up_ref[t, :, :behind] = right_parts(a_ref[tile(t), (t + 1) * 128 :], 0)

            def trail(s, t=t):
                a_ref[tile(s), s * 128 :] -= dot(
                    left_parts(a_ref[tile(t), tile(s)].T, 1),
                    up_ref[t, :, (s - t - 1) * 128 : (3 - t) * 128],
                )

            trail(t + 1)
            work += [functools.partial(trail, s) for s in range(t + 2, 4)]
        work += [functools.partial(solve, t, n) for n in range(PIECES)]
    while work:
        work.pop(0)()
    for copy in copies:
        copy.wait()


def whiten_call(gram, smooth, scale):
    rows = smooth.shape[0]

    def kernel(*refs):
        whiten_kernel(scale, *refs)

    return pl.pallas_call(
        kernel,
        out_shape=jax.ShapeDtypeStruct((rows, BINS), F32),
        in_specs=[
            pl.BlockSpec(memory_space=pltpu.VMEM),
            pl.BlockSpec(memory_space=pl.ANY),
        ],
        out_specs=pl.BlockSpec(memory_space=pl.ANY),
        scratch_shapes=[
            pltpu.VMEM((BINS, BINS), F32),
            pltpu.VMEM((BINS, 128), F32),
            pltpu.VMEM((128, 5 * 128), BF16),
            pltpu.VMEM((4, 128, 6 * 128), BF16),
            pltpu.VMEM((3, 6 * 128, 3 * 128), BF16),
            pltpu.VMEM((rows, BINS), F32),
            pltpu.VMEM((rows, BINS), F32),
            pltpu.SemaphoreType.DMA,
            pltpu.SemaphoreType.DMA((4, PIECES)),
        ],
        compiler_params=pltpu.CompilerParams(vmem_limit_bytes=62 << 20),
    )(gram, smooth)


def local(counts, spread):
    gram, smooth = gram_call(counts, spread.reshape(1, BINS))
    rows_all = smooth.shape[0] * lax.axis_size("gx") * lax.axis_size("gy")
    scores = whiten_call(gram, smooth, math.sqrt(rows_all))
    return scores.reshape(counts.shape)


def solution(mesh):
    in_specs = (P(None, "gx", "gy", None), P())
    out_specs = P(None, "gx", "gy", None)
    return jax.shard_map(local, mesh=mesh, in_specs=in_specs, out_specs=out_specs, check_vma=False)
```

time: 84.4 us -> 76 us (0.900)
  Pallas kernels: 82 us -> 75.7 us
  local copies, waits for them, and re-layouts: 2.27 us -> 0 us
    pallas_call x1, Pallas kernels: 23.8 us -> 17 us  [whiten_call(): pl.pallas_call(kernel, out_shape=jax.ShapeDtypeStruct((rows, BINS), F32),...]
    unnamed x4 -> x0, local copies, waits for them, and re-layouts: 2.27 us -> none
where the time goes in v2:
time: 76 us; the launch traced here: 75.8 us
  Pallas kernels  75.7 us (100%)
    pallas_call x1, Pallas kernels, gram_call(): pl.pallas_call(gram_kernel, out_shape=[jax.ShapeDtypeStruct((PACKED, 128)...  58.6 us
    pallas_call x1, Pallas kernels, whiten_call(): pl.pallas_call(kernel, out_shape=jax.ShapeDtypeStruct((rows, BINS), F32),...  17 us

profile of v2, /device:TPU:1, one launch (start us, length us, event | category | flops | bytes accessed | tf_op | source)
XLA Modules:
  0.0 75.8 jit_solution(11623675208111491322)
XLA Ops:
  0.0 58.6 %shard_map.28 = (f32[1280,128]{1,0:T(8,128)}, f32[1024,512]{1,0:T(8,128)}) custom-call(f32[4,16,16,512]{3,2,1,0:T(8,128)} %counts_ref.1, f32[1,512]{1,0:T(1,128)} %bitcast.2), custom_call_target="tpu_custom_call" | custom-call | tf_op jit(solution)/shard_map/pallas_call | solution.py:469
  58.6 17.0 %shard_map.29 = f32[1024,512]{1,0:T(8,128)} custom-call(f32[1280,128]{1,0:T(8,128)} %get-tuple-element.7.refs_0_, f32[1024,512]{1,0:T(8,128)} %get-tuple-element.8.refs_1_), custom_call_target="tpu_custom_call" | custom-call | tf_op jit(solution)/shard_map/pallas_call | solution.py:664

commit v3 on v2

--- a/solution.py
+++ b/solution.py
@@ -258,7 +258,7 @@
         (from_core0, from_x0, quarter0, from_z0, from_y0, gathered0),
         (from_core1, from_x1, quarter1, from_z1, from_y1, gathered1),
     ]
-    sent = []
+    leaves = []
     gives = []
 
     def reduction(c):
@@ -266,93 +266,89 @@
         half, fourth, eighth = shares(rows)
         from_core, from_x, quarter, from_z, from_y, gathered = buffers[c]
 
-        def send(n, source, target, device):
-            copy = pltpu.make_async_remote_copy(
+        def send(step, source, target, device):
+            pltpu.make_async_remote_copy(
                 src_ref=source,
                 dst_ref=target,
-                send_sem=red_send.at[c, n],
-                recv_sem=red_recv.at[c, n],
+                send_sem=red_send.at[c, step],
+                recv_sem=red_recv.at[c, step],
                 device_id=device,
                 device_id_type=MESH,
-            )
-            copy.start()
-            sent.append(copy)
-            return copy
-
-        copy = send(
-            0, packed.at[rows_at(first + (1 - core) * half, half)], from_core, core_peer()
-        )
+            ).start()
+
+        def arrived(step, landed):
+            pltpu.make_async_copy(landed, landed, red_recv.at[c, step]).wait()
+
+        def left(step, gone):
+            leaves.append(lambda: pltpu.make_async_copy(gone, gone, red_send.at[c, step]).wait())
+
+        send(0, packed.at[rows_at(first + (1 - core) * half, half)], from_core, core_peer())
+        left(0, from_core)
         if fourth < Z_CHIPS * eighth:
             quarter[fourth:, :] = jnp.zeros((Z_CHIPS * eighth - fourth, 128), F32)
         yield
-        copy.wait_recv()
+        arrived(0, from_core)
         mine = first + core * half
         packed[rows_at(mine, half), :] += from_core[...]
 
-        copies = [
+        for d in range(1, X_CHIPS):
             send(
-                d,
+                1,
                 packed.at[rows_at(mine + lax.rem(x + d, X_CHIPS) * fourth, fourth)],
                 from_x.at[d - 1],
                 x_peer(d),
             )
-            for d in range(1, X_CHIPS)
-        ]
+        left(1, from_x)
         yield
-        for copy in copies:
-            copy.wait_recv()
+        arrived(1, from_x)
         total = packed[rows_at(mine + x * fourth, fourth), :]
         for d in range(X_CHIPS - 1):
             total = total + from_x[d]
         quarter[0:fourth, :] = total
 
-        copies = [
+        for d in (4, 3, 5, 2, 6, 1, 7):
             send(
-                3 + d,
+                2,
                 quarter.at[rows_at(lax.rem(z + d, Z_CHIPS) * eighth, eighth)],
                 from_z.at[d - 1],
                 z_peer(d),
             )
-            for d in range(1, Z_CHIPS)
-        ]
+        left(2, from_z)
         yield
-        for copy in copies:
-            copy.wait_recv()
+        arrived(2, from_z)
         total = quarter[rows_at(z * eighth, eighth), :]
         for d in range(Z_CHIPS - 1):
             total = total + from_z[d]
 
         from_y[y] = total
-        copies = [send(10 + d, from_y.at[y], from_y.at[y], y_peer(d)) for d in range(1, Y_CHIPS)]
+        for d in (4, 3, 5, 2, 6, 1, 7):
+            send(3, from_y.at[y], from_y.at[y], y_peer(d))
+        left(3, from_y.at[1:])
         yield
-        for copy in copies:
-            copy.wait_recv()
+        arrived(3, from_y.at[1:])
         total = from_y[0]
         for d in range(1, Y_CHIPS):
             total = total + from_y[d]
 
         here = rows_at(z * eighth, eighth)
         gathered[here, :] = total
-        copies = [
-            send(17 + d, gathered.at[here], gathered.at[here], z_peer(d))
-            for d in range(1, Z_CHIPS)
-        ]
+        for d in (4, 3, 5, 2, 6, 1, 7):
+            send(4, gathered.at[here], gathered.at[here], z_peer(d))
+        left(4, gathered.at[eighth:])
         yield
-        for copy in copies:
-            copy.wait_recv()
+        arrived(4, gathered.at[eighth:])
         here = rows_at(mine + x * fourth, fourth)
-        copies = [
-            send(24 + d, gathered.at[0:fourth], whole.at[here], x_peer(d))
-            for d in range(1, X_CHIPS)
-        ]
+        for d in range(1, X_CHIPS):
+            send(5, gathered.at[0:fourth], whole.at[here], x_peer(d))
+        left(5, from_x)
         whole[here, :] = gathered[0:fourth, :]
         yield
-        for copy in copies:
-            copy.wait_recv()
+        arrived(5, from_x)
         here = rows_at(mine, half)
-        copy = send(28, whole.at[here], whole.at[here], core_peer())
+        send(6, whole.at[here], whole.at[here], core_peer())
+        left(6, from_core)
         yield
-        copy.wait_recv()
+        arrived(6, from_core)
         give = pltpu.make_async_copy(
             whole.at[first : first + rows], gram_ref.at[first : first + rows], out_sems.at[PLANES + c]
         )
@@ -405,8 +401,10 @@
         keeps.append(keep)
 
         value = smooth[rows, :]
-        left = left_parts(value.T, 1)
-        right = right_parts(value, 0)
+        high, middle, _ = split3(value.T)
+        left = jnp.concatenate([high, high, middle, middle], axis=1)
+        high, middle, _ = split3(value)
+        right = jnp.concatenate([high, middle, high, middle], axis=0)
         at = 0
         for i in range(4):
             part = dot(left[tile(i), :], right[:, i * 128 :])
@@ -423,30 +421,30 @@
 
     second_chunk = reduction(1)
     next(second_chunk)
+    for p in range(PLANES):
+        for side in (0, 1):
+
+            @pl.when(there(0, sign[side]))
+            def _():
+                y_copy(p, side).wait_send()
+
+            @pl.when(there(sign[side], 0))
+            def _():
+                x_copy(p, side).wait_send()
+
+        keeps[p].wait()
+    for a in (0, 1):
+        for b in (0, 1):
+
+            @pl.when(there(sign[a], sign[b]))
+            def _():
+                corner_copy(a, b).wait_send()
+
     under_way = [first_chunk, second_chunk]
     while under_way:
         under_way = [chunk for chunk in under_way if next(chunk, chunk) is not chunk]
-    for copy in sent:
-        copy.wait_send()
-    for p in range(PLANES):
-        for side in (0, 1):
-
-            @pl.when(there(0, sign[side]))
-            def _():
-                y_copy(p, side).wait_send()
-
-            @pl.when(there(sign[side], 0))
-            def _():
-                x_copy(p, side).wait_send()
-
-        keeps[p].wait()
-    for a in (0, 1):
-        for b in (0, 1):
-
-            @pl.when(there(sign[a], sign[b]))
-            def _():
-                corner_copy(a, b).wait_send()
-
+    for wait in leaves:
+        wait()
     for give in gives:
         give.wait()
 
@@ -494,8 +492,8 @@
             dma((PLANES, 2)),
             dma((4,)),
             dma((4,)),
-            dma((2, 29)),
-            dma((2, 29)),
+            dma((2, 7)),
+            dma((2, 7)),
             dma((PLANES + 2,)),
         ],
         compiler_params=pltpu.CompilerParams(
@@ -527,11 +525,11 @@
         )
         return value.astype(BF16)
 
-    def lose(rows, left, right):
-        update = dot(left, right)
-        for s in range(width + 1):
+    def lose(rows, left, right, skip=0):
+        update = dot(left, right[:, skip * 128 :])
+        for s in range(skip, width + 1):
             ref, at_rows, columns = at(s, rows)
-            ref[at_rows, columns] -= update[:, tile(s)]
+            ref[at_rows, columns] -= update[:, tile(s - skip)]
 
     for p in range(panels):
         first = t * 128 + p * PANEL
@@ -556,12 +554,19 @@
             beyond = slice(first + PANEL, t * 128 + 128)
             left = column_parts(a_ref[beyond, tile(t)], (p - 1) * PANEL, None)
             lose(beyond, left, parts_ref[:, : (width + 1) * 128])
+        if p < panels - 1:
+            after = slice(first + PANEL, first + 2 * PANEL)
+            below = [a_ref[first + PANEL + 8 * g : first + PANEL + 8 * g + 8, tile(t)] for g in range(2)]
+        under = []
         for j in range(PANEL):
             h, q = divmod(j, 8)
             pivot = jnp.broadcast_to(column[j][h][q : q + 1, :], (8, 128))
             inverse = 1.0 / pivot
             pivots[h] = jnp.where(sublane == q, pivot, pivots[h])
             inverses[h] = jnp.where(sublane == q, inverse, inverses[h])
+            if p < panels - 1:
+                at_lane = jnp.full((8, 128), p * PANEL + j, jnp.int32)
+                under.append([jnp.take_along_axis(value, at_lane, axis=1) * inverse for value in below])
             weight = [
                 (jnp.where(sublane != q, column[j][g], 0.0) if g == h else column[j][g]) * inverse
                 for g in range(2)
@@ -575,7 +580,7 @@
                 kept[h] = jnp.where(sublane == q, other, kept[h])
                 for g in range(2):
                     value[g] = value[g] - weight[g] * other
-            if j in (3, 9) and work:
+            if (j == 6 or (j == 12 and p < 2)) and work:
                 work.pop(0)()
         scale = [lax.rsqrt(value) for value in pivots]
         for s, kept in enumerate(factor):
@@ -592,8 +597,16 @@
             right = right_parts(solved, 0)
             right = jnp.concatenate([right, jnp.zeros((128 - 6 * PANEL, right.shape[1]), BF16)], axis=0)
             parts_ref[:, : (width + 1) * 128] = right
-            after = slice(first + PANEL, first + 2 * PANEL)
-            lose(after, column_parts(a_ref[after, tile(t)], p * PANEL, None), right)
+            for g in range(2):
+                sums = [below[g], None]
+                for j in range(PANEL):
+                    other = jnp.broadcast_to(rows[0][j // 8][j % 8 : j % 8 + 1, :], (8, 128))
+                    term = under[j][g] * other
+                    k = j % 2
+                    sums[k] = -term if sums[k] is None else sums[k] - term
+                low_rows = slice(first + PANEL + 8 * g, first + PANEL + 8 * g + 8)
+                a_ref[low_rows, tile(t)] = sums[0] + sums[1]
+            lose(after, column_parts(jnp.concatenate(below, axis=0), p * PANEL, None), right, 1)
     while work:
         work.pop(0)()
 

time: 76 us -> 71.5 us (0.941)
  Pallas kernels: 75.7 us -> 71.1 us
    pallas_call x1, Pallas kernels: 17 us -> 14.6 us  [whiten_call(): pl.pallas_call(kernel, out_shape=jax.ShapeDtypeStruct((rows, BINS), F32),...]
    pallas_call x1, Pallas kernels: 58.6 us -> 56.6 us  [gram_call(): pl.pallas_call(gram_kernel, out_shape=[jax.ShapeDtypeStruct((PACKED, 128)...]
where the time goes in v3:
time: 71.5 us; the launch traced here: 71.3 us
  Pallas kernels  71.1 us (99%)
    pallas_call x1, Pallas kernels, gram_call(): pl.pallas_call(gram_kernel, out_shape=[jax.ShapeDtypeStruct((PACKED, 128)...  56.6 us
    pallas_call x1, Pallas kernels, whiten_call(): pl.pallas_call(kernel, out_shape=jax.ShapeDtypeStruct((rows, BINS), F32),...  14.6 us

profile of v3, /device:TPU:1, one launch (start us, length us, event | category | flops | bytes accessed | tf_op | source)
XLA Modules:
  0.0 71.3 jit_solution(3208396184353996265)
XLA Ops:
  0.0 56.6 %shard_map.28 = (f32[1280,128]{1,0:T(8,128)}, f32[1024,512]{1,0:T(8,128)}) custom-call(f32[4,16,16,512]{3,2,1,0:T(8,128)} %counts_ref.1, f32[1,512]{1,0:T(1,128)} %bitcast.2), custom_call_target="tpu_custom_call" | custom-call | tf_op jit(solution)/shard_map/pallas_call | solution.py:467
  56.6 14.6 %shard_map.29 = f32[1024,512]{1,0:T(8,128)} custom-call(f32[1280,128]{1,0:T(8,128)} %get-tuple-element.7.refs_0_, f32[1024,512]{1,0:T(8,128)} %get-tuple-element.8.refs_1_), custom_call_target="tpu_custom_call" | custom-call | tf_op jit(solution)/shard_map/pallas_call | solution.py:677

commit v4 on v3

--- a/solution.py
+++ b/solution.py
@@ -244,6 +244,20 @@
     taps_load.wait()
     taps = tap_rows(taps_in[...])
 
+    def along_x(p, i, lo, hi):
+        total = taps[0] * grid[p, i, lo:hi, :]
+        for k in range(1, 2 * RADIUS + 1):
+            total = total + taps[k] * grid[p, i + k, lo:hi, :]
+        blurred[p, i, lo:hi, :] = total
+
+    for p in range(PLANES):
+
+        def inner_x(i, carry, p=p):
+            along_x(p, i, 8, 8 + SIDE)
+            return carry
+
+        lax.fori_loop(RADIUS, SIDE - RADIUS, inner_x, 0)
+
     for a in (0, 1):
         for b in (0, 1):
 
@@ -376,20 +390,19 @@
                         2 * a + b, 4 * p + 2 * i : 4 * p + 2 * i + 2, :
                     ]
 
-        def along_x(i, carry, p=p):
-            for lo, hi in ((0, 8), (8, 24), (24, 32)):
-                total = taps[0] * grid[p, i, lo:hi, :]
-                for k in range(1, 2 * RADIUS + 1):
-                    total = total + taps[k] * grid[p, i + k, lo:hi, :]
-                blurred[i, lo:hi, :] = total
+        def beside_x(i, carry, p=p):
+            along_x(p, i, 0, 8)
+            along_x(p, i, 8 + SIDE, 16 + SIDE)
             return carry
 
-        lax.fori_loop(0, SIDE, along_x, 0)
+        lax.fori_loop(0, SIDE, beside_x, 0)
+        for i in (0, 1, SIDE - 2, SIDE - 1):
+            along_x(p, i, 8, 8 + SIDE)
 
         def along_y(i, carry, p=p):
-            total = taps[0] * blurred[i, 6 : 6 + SIDE, :]
+            total = taps[0] * blurred[p, i, 6 : 6 + SIDE, :]
             for k in range(1, 2 * RADIUS + 1):
-                total = total + taps[k] * blurred[i, 6 + k : 6 + k + SIDE, :]
+                total = total + taps[k] * blurred[p, i, 6 + k : 6 + k + SIDE, :]
             at = pl.multiple_of(p * SIDE * SIDE + i * SIDE, SIDE)
             smooth[pl.ds(at, SIDE), :] = total
             return carry
@@ -474,7 +487,7 @@
         out_specs=[pl.BlockSpec(memory_space=pl.ANY)] * 2,
         scratch_shapes=[
             pltpu.VMEM((PLANES, SIDE + 2 * RADIUS, SIDE + 16, BINS), F32),
-            pltpu.VMEM((SIDE, SIDE + 16, BINS), F32),
+            pltpu.VMEM((PLANES, SIDE, SIDE + 16, BINS), F32),
             pltpu.VMEM((rows, BINS), F32),
             pltpu.VMEM((2, PLANES, 2 * SIDE, BINS), F32),
             pltpu.VMEM((2, PLANES, 2 * SIDE, BINS), F32),

time: 71.5 us -> 71 us (level)
  no operation moved by 1% of the time
where the time goes in v4:
time: 71 us; the launch traced here: 70.8 us
  Pallas kernels  70.7 us (100%)
    pallas_call x1, Pallas kernels, gram_call(): pl.pallas_call(gram_kernel, out_shape=[jax.ShapeDtypeStruct((PACKED, 128)...  56.1 us
    pallas_call x1, Pallas kernels, whiten_call(): pl.pallas_call(kernel, out_shape=jax.ShapeDtypeStruct((rows, BINS), F32),...  14.6 us

profile of v4, /device:TPU:1, one launch (start us, length us, event | category | flops | bytes accessed | tf_op | source)
XLA Modules:
  0.0 70.8 jit_solution(11676847941925338751)
XLA Ops:
  0.0 56.1 %shard_map.28 = (f32[1280,128]{1,0:T(8,128)}, f32[1024,512]{1,0:T(8,128)}) custom-call(f32[4,16,16,512]{3,2,1,0:T(8,128)} %counts_ref.1, f32[1,512]{1,0:T(1,128)} %bitcast.2), custom_call_target="tpu_custom_call" | custom-call | tf_op jit(solution)/shard_map/pallas_call | solution.py:480
  56.1 14.6 %shard_map.29 = f32[1024,512]{1,0:T(8,128)} custom-call(f32[1280,128]{1,0:T(8,128)} %get-tuple-element.7.refs_0_, f32[1024,512]{1,0:T(8,128)} %get-tuple-element.8.refs_1_), custom_call_target="tpu_custom_call" | custom-call | tf_op jit(solution)/shard_map/pallas_call | solution.py:690

commit v5 on v4

--- a/solution.py
+++ b/solution.py
@@ -369,6 +369,10 @@
         give.start()
         gives.append(give)
 
+    squares = jnp.zeros((1, BINS), F32)
+    diagonal = lax.broadcasted_iota(jnp.int32, (128, 128), 0) == lax.broadcasted_iota(
+        jnp.int32, (128, 128), 1
+    )
     keeps = []
     for p in range(PLANES):
         for side in (0, 1):
@@ -415,14 +419,18 @@
 
         value = smooth[rows, :]
         high, middle, _ = split3(value.T)
-        left = jnp.concatenate([high, high, middle, middle], axis=1)
+        left = jnp.concatenate([high, high, middle], axis=1)
         high, middle, _ = split3(value)
-        right = jnp.concatenate([high, middle, high, middle], axis=0)
+        right = jnp.concatenate([high, middle, high], axis=0)
+        middle = middle.astype(F32)
+        squares = squares + jnp.sum(middle * middle, axis=0, keepdims=True)
         at = 0
         for i in range(4):
             part = dot(left[tile(i), :], right[:, i * 128 :])
             for j in range(4 - i):
                 block = part[:, tile(j)]
+                if p == PLANES - 1 and j == 0:
+                    block = block + jnp.where(diagonal, squares[:, tile(i)], 0.0)
                 if p == 0:
                     packed[at : at + 128, :] = block
                 else:

time: 71 us -> 71 us (level)
  no operation moved by 1% of the time
where the time goes in v5:
time: 71 us; the launch traced here: 70.8 us
  Pallas kernels  70.7 us (100%)
    pallas_call x1, Pallas kernels, gram_call(): pl.pallas_call(gram_kernel, out_shape=[jax.ShapeDtypeStruct((PACKED, 128)...  56.1 us
    pallas_call x1, Pallas kernels, whiten_call(): pl.pallas_call(kernel, out_shape=jax.ShapeDtypeStruct((rows, BINS), F32),...  14.6 us

profile of v5, /device:TPU:1, one launch (start us, length us, event | category | flops | bytes accessed | tf_op | source)
XLA Modules:
  0.0 70.8 jit_solution(7606363567711297789)
XLA Ops:
  0.0 56.1 %shard_map.28 = (f32[1280,128]{1,0:T(8,128)}, f32[1024,512]{1,0:T(8,128)}) custom-call(f32[4,16,16,512]{3,2,1,0:T(8,128)} %counts_ref.1, f32[1,512]{1,0:T(1,128)} %bitcast.2), custom_call_target="tpu_custom_call" | custom-call | tf_op jit(solution)/shard_map/pallas_call | solution.py:488
  56.1 14.6 %shard_map.29 = f32[1024,512]{1,0:T(8,128)} custom-call(f32[1280,128]{1,0:T(8,128)} %get-tuple-element.7.refs_0_, f32[1024,512]{1,0:T(8,128)} %get-tuple-element.8.refs_1_), custom_call_target="tpu_custom_call" | custom-call | tf_op jit(solution)/shard_map/pallas_call | solution.py:698

commit v6 on v4

--- a/solution.py
+++ b/solution.py
@@ -625,12 +625,17 @@
 
 
 def whiten_kernel(
-    scale, gram_ref, smooth_ref, scores_ref, a_ref, w_ref, parts_ref, wp_ref, up_ref, left_ref, scores, load_sem, out_sems
+    scale, gram_ref, smooth_ref, scores_ref, a_ref, w_ref, parts_ref, wp_ref, up_ref, left_ref, scores, load_sem, block_sems, out_sems
 ):
+    blocks = []
+    for n, (i, j) in enumerate(BLOCKS):
+        block = pltpu.make_async_copy(
+            gram_ref.at[tile(n), :], a_ref.at[tile(i), tile(j)], block_sems.at[n]
+        )
+        block.start()
+        blocks.append(block)
     load = pltpu.make_async_copy(smooth_ref, left_ref, load_sem)
     load.start()
-    for n, (i, j) in enumerate(BLOCKS):
-        a_ref[tile(i), tile(j)] = gram_ref[tile(n), :]
     size = left_ref.shape[0] // PIECES
     copies = []
 
@@ -658,8 +663,13 @@
     work = []
     for t in range(4):
         w_ref[tile(t), :] = identity
+        if t == 0:
+            for block in blocks[:4]:
+                block.wait()
         factor_block(t, a_ref, w_ref, parts_ref, work)
         if t == 0:
+            for block in blocks[4:]:
+                block.wait()
             load.wait()
         wp_ref[t] = right_parts(w_ref[tile(t), :], 1)
         if t < 3:
@@ -690,10 +700,7 @@
     return pl.pallas_call(
         kernel,
         out_shape=jax.ShapeDtypeStruct((rows, BINS), F32),
-        in_specs=[
-            pl.BlockSpec(memory_space=pltpu.VMEM),
-            pl.BlockSpec(memory_space=pl.ANY),
-        ],
+        in_specs=[pl.BlockSpec(memory_space=pl.ANY)] * 2,
         out_specs=pl.BlockSpec(memory_space=pl.ANY),
         scratch_shapes=[
             pltpu.VMEM((BINS, BINS), F32),
@@ -704,6 +711,7 @@
             pltpu.VMEM((rows, BINS), F32),
             pltpu.VMEM((rows, BINS), F32),
             pltpu.SemaphoreType.DMA,
+            pltpu.SemaphoreType.DMA((len(BLOCKS),)),
             pltpu.SemaphoreType.DMA((4, PIECES)),
         ],
         compiler_params=pltpu.CompilerParams(vmem_limit_bytes=62 << 20),

time: 71 us -> 70.9 us (level)
  no operation moved by 1% of the time
where the time goes in v6:
time: 70.9 us; the launch traced here: 70.8 us
  Pallas kernels  70.6 us (100%)
    pallas_call x1, Pallas kernels, gram_call(): pl.pallas_call(gram_kernel, out_shape=[jax.ShapeDtypeStruct((PACKED, 128)...  56.1 us
    pallas_call x1, Pallas kernels, whiten_call(): pl.pallas_call(kernel, out_shape=jax.ShapeDtypeStruct((rows, BINS), F32),...  14.5 us

profile of v6, /device:TPU:1, one launch (start us, length us, event | category | flops | bytes accessed | tf_op | source)
XLA Modules:
  0.0 70.8 jit_solution(12162411925403020315)
XLA Ops:
  0.0 56.1 %shard_map.28 = (f32[1280,128]{1,0:T(8,128)}, f32[1024,512]{1,0:T(8,128)}) custom-call(f32[4,16,16,512]{3,2,1,0:T(8,128)} %counts_ref.1, f32[1,512]{1,0:T(1,128)} %bitcast.2), custom_call_target="tpu_custom_call" | custom-call | tf_op jit(solution)/shard_map/pallas_call | solution.py:480
  56.1 14.5 %shard_map.29 = f32[1024,512]{1,0:T(8,128)} custom-call(f32[1280,128]{1,0:T(8,128)} %get-tuple-element.7.refs_0_, f32[1024,512]{1,0:T(8,128)} %get-tuple-element.8.refs_1_), custom_call_target="tpu_custom_call" | custom-call | tf_op jit(solution)/shard_map/pallas_call | solution.py:700
